TPU v7x, 32 devices: a whole 2x2x4 slice. The times are simulated.
32 devices in a mesh: group: 2 (over x), blk: 16 (over z, y, core).
Axes of the slice: x: 2, y: 2, z: 4, core: 2. Of those that a mesh axis runs over, the one named last changes fastest.
Arguments:
- adjoint: float32 [10, 256, 8, 128], P('group', 'blk'), parts along dimension 0, may hold values from -6 to 6
- jac_diag: float32 [10, 5, 256, 8, 128], P('group', None, 'blk'), parts along dimension 0, may hold values from -2.5 to 2.5
- conv_mats: float32 [3, 5, 5], replicated, may hold values from -2.5 to 2.5
- face_scale: float32 [6, 256, 8, 128], P('group', 'blk'), parts along dimension 0, may hold values from 0.5 to 2
- kappa: float32 [512, 8, 128], P(('group', 'blk')), parts along dimension 0, may hold values from 0.1 to 1
- source: float32 [10, 256, 8, 128], P('group', 'blk'), parts along dimension 0, may hold values from -6 to 6
- box_of_row: int32 [65536, 1], P(('group', 'blk')), parts along dimension 0, may hold values from 0 to 15; in each aligned block of 2048 rows (0 to 2047, 2048 to 4095, ...) at most 256 rows name the same one
- lattice_cell: int32 [65536], P(('group', 'blk')), parts along dimension 0, may hold values from 0 to 3374
- lattice_frac: float32 [3, 65536], P(None, ('group', 'blk')), parts along dimension 1, may hold values from 0 to 1
- dres_dx: float32 [5, 3, 65536], P(None, None, ('group', 'blk')), parts along dimension 2, may hold values from -2.5 to 2.5
- dobj_dx: float32 [3, 65536], P(None, ('group', 'blk')), parts along dimension 1, may hold values from -6 to 6
Outputs:
- residual: float32 [10, 256, 8, 128], P('group', 'blk'), parts along dimension 0
- box_sens: float32 [6, 65536], P('group', 'blk'), parts along dimension 0
There are 2 independent parts, one for each index of `group`. A program takes and returns all parts, laid end to end along the dimension named above; an argument that names none is the same for every part. Nothing has to cross between parts.
Inputs may be any that keep to these rules, and one draw needn't show every extreme that they name: `box_of_row`: among the 2048 rows of one device no box is named more than 256 times, one box exactly 256 times in some devices' rows; every box is named somewhere.
All inputs are finite; a program needn't handle non-finite values.
Results may differ from a plain program's by a relative error of at most 0.0003.
Values sent between devices are 32-bit elements; how exact they have to be, the bound alone decides.
No kernel may reach another device: no remote copies, remote signals or barrier semaphores. Data moves between devices by JAX's collectives and lax.ppermute only.
A program may use at most 320 MiB of HBM per device.

v0:
```python
import jax
import jax.numpy as jnp
from jax import lax
from jax.sharding import PartitionSpec as P

LAT = 16


def with_halo(cells, sides, width):
    for axis, dim in sides:
        count = lax.axis_size(axis)
        ends = count - 1
        head = lax.slice_in_dim(cells, 0, width, axis=dim)
        tail = lax.slice_in_dim(cells, cells.shape[dim] - width, cells.shape[dim], axis=dim)
        cells = jnp.concatenate(
            [
                lax.ppermute(tail, axis, [(i, (i + 1) % count) for i in range(ends)]),
                cells,
                lax.ppermute(head, axis, [((i + 1) % count, i) for i in range(ends)]),
            ],
            axis=dim,
        )
    return cells


def neighbour(arr, dim, off):
    parts = [slice(1, -1), slice(1, -1), slice(1, -1)]
    parts[dim] = slice(1 + off, arr.shape[dim + 1] - 1 + off)
    return arr[(slice(None),) + tuple(parts)]


def small_apply(coeff, fields):
    count = fields.shape[0]
    rows = []
    for out_index in range(count):
        total = coeff[0, out_index] * fields[0]
        for in_index in range(1, count):
            total = total + coeff[in_index, out_index] * fields[in_index]
        rows.append(total)
    return jnp.stack(rows, 0)


def sweep(padded, jac_diag, conv_mats, face_scale, source):
    psi_pad = padded[:-1]
    kap_pad = padded[-1:]
    centre = neighbour(psi_pad, 0, 0)
    kap_centre = neighbour(kap_pad, 0, 0)
    result = small_apply(jac_diag, centre)
    for direction in range(3):
        upper = neighbour(psi_pad, direction, 1)
        lower = neighbour(psi_pad, direction, -1)
        flux = small_apply(conv_mats[direction], upper - lower)
        result = result + 0.5 * face_scale[direction][None] * flux
        for off, beside in ((1, upper), (-1, lower)):
            weight = 0.5 * (kap_centre + neighbour(kap_pad, direction, off))
            result = result - weight * (beside - centre)
    return result - source


def corner_terms(sens, cell, frac):
    edge = LAT
    inner = LAT - 1
    first = cell // (inner * inner)
    second = cell // inner % inner
    third = cell % inner
    ids = []
    vals = []
    for step_a in (0, 1):
        for step_b in (0, 1):
            for step_c in (0, 1):
                ids.append(
                    (first + step_a) * edge * edge + (second + step_b) * edge + third + step_c
                )
                weight_a = frac[0] if step_a else 1.0 - frac[0]
                weight_b = frac[1] if step_b else 1.0 - frac[1]
                weight_c = frac[2] if step_c else 1.0 - frac[2]
                vals.append(sens * (weight_a * weight_b * weight_c)[None])
    return (jnp.stack(ids, 0), jnp.stack(vals, 1))


def local(
    adjoint,
    jac_diag,
    conv_mats,
    face_scale,
    kappa,
    source,
    box_of_row,
    lattice_cell,
    lattice_frac,
    dres_dx,
    dobj_dx,
):
    stacked = jnp.concatenate([adjoint, kappa[None]], 0)
    extended = with_halo(stacked, (("blk", 1),), 1)
    padded = jnp.pad(extended, ((0, 0), (0, 0), (1, 1), (1, 1)))
    residual = sweep(padded, jac_diag, conv_mats, face_scale, source)
    wall_psi = adjoint[:, :, 0, :].reshape(adjoint.shape[0], -1)
    partial_value = dres_dx[0] * wall_psi[0][None]
    for index in range(1, wall_psi.shape[0]):
        partial_value = partial_value + dres_dx[index] * wall_psi[index][None]
    sens = dobj_dx - partial_value
    box_count = lax.axis_size("blk")
    points = LAT**3
    boxes = box_of_row[:, 0]
    ids, vals = corner_terms(sens, lattice_cell, lattice_frac)
    target = (boxes[None, :] * points + ids).reshape(-1)
    tiles = jnp.zeros((3, box_count * points), jnp.float32).at[:, target].add(vals.reshape(3, -1))
    box_sens = lax.psum_scatter(tiles, "blk", scatter_dimension=1, tiled=True)
    return (residual, box_sens)


def solution(mesh):
    in_specs = (
        P("group", "blk", None, None),
        P("group", None, "blk", None, None),
        P(),
        P("group", "blk", None, None),
        P(("group", "blk"), None, None),
        P("group", "blk", None, None),
        P(("group", "blk"), None),
        P(("group", "blk")),
        P(None, ("group", "blk")),
        P(None, None, ("group", "blk")),
        P(None, ("group", "blk")),
    )
    out_specs = (P("group", "blk", None, None), P("group", "blk"))
    return jax.shard_map(local, mesh=mesh, in_specs=in_specs, out_specs=out_specs, check_vma=False)
```

profile of v0, /device:TPU:0, one launch (start us, length us, event | category | flops | bytes accessed | tf_op | source)
XLA Modules:
  0.0 464.2 jit_solution(7311897239789366240)
XLA Ops:
  7.2 0.0 reduce-scatter.2.cloned.1.call-start
  7.2 0.9 fusion.54
  8.1 0.9 multiply_multiply_fusion
  9.0 1.0 fusion.56
  10.0 0.9 constant_dynamic-update-slice_fusion.7
  11.1 0.0 copy-start.5
  11.1 0.0 copy-start.6
  11.1 5.1 %copy.20 = f32[16384,3]{1,0:T(8,128)} copy(f32[16384,3]{0,1:T(4,128)S(1)} %bitcast.329) | data formatting | bytes 393216 | tf_op jit(solution)/shard_map/reshape | solution.py:108
  16.2 0.1 stack.98
  16.4 0.1 copy.25
  16.4 0.1 compare_select_fusion
  16.5 100.8 %scatter_custom_fusion = f32[3,65536]{0,1:T(8,128)} fusion(s32[16384]{0:T(1024)S(1)} %bitcast.333, f32[16384,3]{1,0:T(8,128)} %copy.20, f32[]{:T(128)} %constant.37.clone.1), kind=kCustom, calls=%fused_computation.1 | custom fusion | flops 49152 | bytes 786944 | tf_op jit(solution)/shard_map/scatter-add | solution.py:108
  117.3 0.0 reduce-scatter.2.cloned.1.call-update
  117.3 0.9 copy-done
  118.3 1.3 collective-permute-start
  119.6 3.0 collective-permute-start.1
  122.6 0.6 fusion.59
  123.3 0.7 fusion.58
  124.0 0.6 fusion.61
  124.7 0.7 fusion.60
  125.4 0.7 fusion.62
  126.2 0.6 fusion.63
  126.8 0.5 select_maximum_fusion
  127.3 0.3 slice_subtract_fusion.1
  127.6 0.7 copy-done.2
  128.3 0.1 fusion.16
  128.4 0.1 pad_maximum_fusion
  128.5 0.1 slice_subtract_fusion.2
  128.5 3.0 add_dynamic-update-slice_fusion.14
  131.6 3.1 add_dynamic-update-slice_fusion.13
  134.7 3.2 add_dynamic-update-slice_fusion.12
  137.9 3.2 add_dynamic-update-slice_fusion.11
  141.1 3.1 add_dynamic-update-slice_fusion.10
  144.2 3.2 add_dynamic-update-slice_fusion.9
  147.3 3.3 add_dynamic-update-slice_fusion.8
  150.6 3.1 add_dynamic-update-slice_fusion.7
  153.7 3.1 add_dynamic-update-slice_fusion.6
  156.8 2.9 add_dynamic-update-slice_fusion.5
  159.8 3.0 add_dynamic-update-slice_fusion.4
  162.8 0.0 copy-start.3
  162.8 3.3 add_dynamic-update-slice_fusion.3
  166.1 3.0 add_dynamic-update-slice_fusion.2
  169.1 3.1 add_dynamic-update-slice_fusion.1
  172.2 3.3 add_dynamic-update-slice_fusion
  175.6 0.1 fusion.12
  175.8 1.2 subtract_subtract_fusion
  177.0 277.6 %reduce-scatter.2.cloned.1.call-done = f32[3,4096]{0,1:T(8,128)} async-done(((f32[3,65536]{0,1:T(8,128)}), f32[3,4096]{0,1:T(8,128)}) %reduce-scatter.2.cloned.1.call-update) | async-done | bytes 49168 | tf_op jit(solution)/shard_map/reduce_scatter | solution.py:109
  454.5 2.8 copy.21
  (32 shorter events, 0.4 us)
Async XLA Ops:
  7.2 447.4 %reduce-scatter.2.cloned.1.call-start = ((), (), s32[]{:S(2)}) async-start(), calls=%async_computation.1 | async-start | bytes 35651584 | tf_op jit(solution)/shard_map/reduce_scatter | solution.py:109
  11.1 5.1 %copy-start.5 = (s32[2048]{0:T(1024)S(1)}, s32[2048]{0:T(1024)}, u32[]{:S(2)}) copy-start(s32[2048]{0:T(1024)} %param.18) | copy-start | bytes 24580
  11.1 5.1 %copy-start.6 = (s32[2048,1]{0,1:T(1,128)S(1)}, s32[2048,1]{0,1:T(1,128)}, u32[]{:S(2)}) copy-start(s32[2048,1]{0,1:T(1,128)} %param.17) | copy-start | bytes 24580
  117.3 1.0 copy-start
  117.3 1.0 copy-start.1
  117.3 5.3 %copy-start.7 = (f32[3,5,5]{2,0,1:T(4,128)S(1)}, f32[3,5,5]{2,0,1:T(4,128)}, u32[]{:S(2)}) copy-start(f32[3,5,5]{2,0,1:T(4,128)} %param.13) | copy-start | bytes 904
  117.3 8.8 %copy-start.4 = (f32[3,16,8,128]{3,2,1,0:T(8,128)S(1)}, f32[3,16,8,128]{3,2,1,0:T(8,128)}, u32[]{:S(2)}) copy-start(f32[3,16,8,128]{3,2,1,0:T(8,128)} %param.14) | copy-start | bytes 589828
  118.3 8.5 %collective-permute-start = (f32[6,1,8,128]{3,2,1,0:T(8,128)S(1)}, f32[6,1,8,128]{3,2,1,0:T(8,128)S(1)}, u32[]{:S(2)}, u32[]{:S(2)}) collective-permute-start(f32[6,1,8,128]{3,2,1,0:T(8,128)S(1)} %get-tuple-element.27), channel_id=1, source_target_pairs={{1,0},{2,1},{3,2},{4,3},{5,4},{6,5},{7,6},{8,7},{9,8},{10,9},{11,1... | collective-permute-start | bytes 73736 | tf_op jit(solution)/shard_map/ppermute | solution.py:19
  119.6 7.2 %collective-permute-start.1 = (f32[6,1,8,128]{3,2,1,0:T(8,128)S(1)}, f32[6,1,8,128]{3,2,1,0:T(8,128)S(1)}, u32[]{:S(2)}, u32[]{:S(2)}) collective-permute-start(f32[6,1,8,128]{3,2,1,0:T(8,128)S(1)} %get-tuple-element.26), channel_id=1, source_target_pairs={{0,1},{1,2},{2,3},{3,4},{4,5},{5,6},{6,7},{7,8},{8,9},{9,10},{10,1... | collective-permute-start | bytes 73736 | tf_op jit(solution)/shard_map/ppermute | solution.py:17
  126.7 1.5 copy-start.2
  162.8 13.0 %copy-start.3 = (f32[5,16,8,128]{3,2,1,0:T(8,128)S(1)}, f32[5,16,8,128]{3,2,1,0:T(8,128)}, u32[]{:S(2)}) copy-start(f32[5,16,8,128]{3,2,1,0:T(8,128)} %param.16) | copy-start | bytes 983044
Sparse Core Ops, SparseCore 0:
  117.5 337.0 reduce-scatter.1
where the time goes:
time: 465 us; the launch traced here: 464 us
  waiting for transfers between devices  278 us (60%)
  other arithmetic  153 us (33%)
  local copies, waits for them, and re-layouts  14.7 us (3%)
  between operations  14.4 us (3%)
    reduce_scatter x1, waiting for transfers between devices, local(): box_sens = lax.psum_scatter(tiles, 'blk', scatter_dimension=1, tiled=True)  278 us
    scatter-add x1, other arithmetic, local(): jnp.zeros((3, box_count * points), jnp.float32).at[:, target]  101 us
    unnamed x23, other arithmetic  38.7 us
    another operation x4, other arithmetic, small_apply(): return jnp.stack(rows, 0)  9.37 us
  transfers between devices with their start and end apart: 3, of which 1 were waited for; matrix products, arithmetic and copies ran while one was open for 12% of the time, Pallas kernels for 0%

commit v1 on v0

v1 whole, which is shorter than its diff:
```python
import functools

import jax
import jax.numpy as jnp
from jax import lax
from jax.experimental import pallas as pl
from jax.experimental.pallas import tpu as pltpu
from jax.sharding import PartitionSpec as P

LAT = 16
CHUNK = 256
F32 = jnp.float32
BF16 = jnp.bfloat16
NT = (((1,), (1,)), ((), ()))
NN = (((1,), (0,)), ((), ()))


def split_two(x):
    hi = x.astype(BF16)
    lo = (x - hi.astype(F32)).astype(BF16)
    return hi, lo


def pack_kernel(boxes, cap, adj_ref, box_ref, cell_ref, frac_ref, dres_ref, dobj_ref, out_ref, ranks_ref):
    fields, planes, _, lanes = adj_ref.shape
    rows = planes * lanes
    box = box_ref[...]

    chunks = rows // CHUNK
    names = lax.broadcasted_iota(jnp.int32, (boxes, CHUNK), 0)
    hot = [(box[:, j * CHUNK:(j + 1) * CHUNK] == names).astype(F32) for j in range(chunks)]
    earlier = (
        lax.broadcasted_iota(jnp.int32, (CHUNK, CHUNK), 0)
        < lax.broadcasted_iota(jnp.int32, (CHUNK, CHUNK), 1)
    ).astype(F32).astype(BF16)
    counts = lax.dot_general(
        jnp.concatenate(hot, 0).astype(BF16), earlier, NN, preferred_element_type=F32
    )
    offset = jnp.zeros((boxes, 1), F32)
    for j in range(chunks):
        here = counts[j * boxes:(j + 1) * boxes]
        ranks_ref[:, j * CHUNK:(j + 1) * CHUNK] = jnp.sum(
            hot[j] * (here + offset), axis=0, keepdims=True
        )
        offset = offset + here[:, CHUNK - 1:] + hot[j][:, CHUNK - 1:]

    total = jnp.zeros((boxes * 16, cap), F32)
    slots = lax.broadcasted_iota(jnp.int32, (cap, CHUNK), 0).astype(F32)
    per = CHUNK // lanes
    for j in range(chunks):
        part = slice(j * CHUNK, (j + 1) * CHUNK)
        acc = dobj_ref[:, part]
        for k in range(fields):
            psi = jnp.concatenate(
                [adj_ref[k, x, 0:1, :] for x in range(j * per, (j + 1) * per)], 1
            )
            acc = acc - dres_ref[k, :, part] * psi
        values = jnp.concatenate(
            [acc, frac_ref[:, part], cell_ref[:, part].astype(F32), jnp.zeros((1, CHUNK), F32)], 0
        )
        hi = values.astype(BF16).astype(F32)
        both = jnp.concatenate([hi, values - hi], 0)
        mine = box[:, part]
        lhs = jnp.concatenate(
            [jnp.where(mine == b, both, 0.0) for b in range(boxes)], 0
        ).astype(BF16)
        rhs = (slots == ranks_ref[:, part]).astype(F32).astype(BF16)
        total = total + lax.dot_general(lhs, rhs, NT, preferred_element_type=F32)
    for b in range(boxes):
        out_ref[b] = total[b * 16:b * 16 + 8] + total[b * 16 + 8:b * 16 + 16]


def sum_kernel(got_ref, out_ref):
    sources, _, cap = got_ref.shape
    inner = LAT - 1
    points = lax.broadcasted_iota(jnp.int32, (LAT, cap), 0).astype(F32)
    both = jnp.zeros((6 * LAT, LAT * LAT), F32)
    for s in range(sources):
        block = got_ref[s]
        cell = block[6:7]
        first = jnp.floor((cell + 0.5) * (1.0 / (inner * inner)))
        rest = cell - first * (inner * inner)
        second = jnp.floor((rest + 0.5) * (1.0 / inner))
        third = rest - second * inner
        tent = []
        for d, low in enumerate((first, second, third)):
            u = block[3 + d:4 + d]
            tent.append(
                jnp.where(points == low, 1.0 - u, 0.0) + jnp.where(points == low + 1.0, u, 0.0)
            )
        left = jnp.concatenate([tent[0] * block[c:c + 1] for c in range(3)], 0)
        right = jnp.concatenate([tent[1][b:b + 1] * tent[2] for b in range(LAT)], 0)
        left_hi, left_lo = split_two(left)
        right_hi, right_lo = split_two(right)
        lhs = jnp.concatenate([left_hi, left_lo], 0)
        both = both + lax.dot_general(lhs, right_hi, NT, preferred_element_type=F32)
        both = both + lax.dot_general(lhs, right_lo, NT, preferred_element_type=F32)
    result = both[:3 * LAT] + both[3 * LAT:]
    for c in range(3):
        for a in range(LAT):
            out_ref[c:c + 1, a * LAT * LAT:(a + 1) * LAT * LAT] = result[c * LAT + a:c * LAT + a + 1]


def sweep_kernel(conv_ref, adj_ref, jac_ref, face_ref, kap_ref, src_ref, low_ref, high_ref, out_ref):
    fields, planes, rows, lanes = adj_ref.shape
    row = lax.broadcasted_iota(jnp.int32, (rows, lanes), 0)
    lane = lax.broadcasted_iota(jnp.int32, (rows, lanes), 1)
    keep = (
        (row < rows - 1, row > 0),
        (lane < lanes - 1, lane > 0),
    )

    def at(field, x):
        if x < 0:
            return low_ref[field, 0]
        if x == planes:
            return high_ref[field, 0]
        return adj_ref[field, x] if field < fields else kap_ref[x]

    def shifted(value, dim):
        size = value.shape[dim]
        up = jnp.where(keep[dim][0], pltpu.roll(value, size - 1, dim), 0.0)
        down = jnp.where(keep[dim][1], pltpu.roll(value, 1, dim), 0.0)
        return up, down

    for x in range(planes):
        centre = [at(f, x) for f in range(fields)]
        kap = at(fields, x)
        result = []
        for f in range(fields):
            total = jac_ref[0, f, x] * centre[0]
            for k in range(1, fields):
                total = total + jac_ref[k, f, x] * centre[k]
            result.append(total - src_ref[f, x])
        for direction in range(3):
            if direction == 0:
                pair = [(at(f, x + 1), at(f, x - 1)) for f in range(fields + 1)]
            else:
                pair = [shifted(v, direction - 1) for v in centre + [kap]]
            scale = 0.5 * face_ref[direction, x]
            diff = [scale * (pair[k][0] - pair[k][1]) for k in range(fields)]
            up = 0.5 * (kap + pair[fields][0])
            down = 0.5 * (kap + pair[fields][1])
            for f in range(fields):
                total = result[f]
                for k in range(fields):
                    total = total + conv_ref[(direction * fields + k) * fields + f] * diff[k]
                total = total - up * (pair[f][0] - centre[f]) - down * (pair[f][1] - centre[f])
                result[f] = total
        for f in range(fields):
            out_ref[f, x] = result[f]


def local(
    adjoint,
    jac_diag,
    conv_mats,
    face_scale,
    kappa,
    source,
    box_of_row,
    lattice_cell,
    lattice_frac,
    dres_dx,
    dobj_dx,
):
    boxes = lax.axis_size("blk")
    rows = box_of_row.shape[0]
    cap = 2 * rows // boxes
    vmem = pl.BlockSpec(memory_space=pltpu.VMEM)
    smem = pl.BlockSpec(memory_space=pltpu.SMEM)

    ends = boxes - 1
    stacked = jnp.concatenate([adjoint, kappa[None]], 0)
    low = lax.ppermute(stacked[:, -1:], "blk", [(i, i + 1) for i in range(ends)])
    high = lax.ppermute(stacked[:, :1], "blk", [(i + 1, i) for i in range(ends)])

    packed = pl.pallas_call(
        functools.partial(pack_kernel, boxes, cap),
        out_shape=jax.ShapeDtypeStruct((boxes, 8, cap), F32),
        in_specs=[vmem] * 6,
        out_specs=vmem,
        scratch_shapes=[pltpu.VMEM((1, rows), F32)],
        name="pack_rows",
    )(
        adjoint,
        box_of_row.reshape(1, rows),
        lattice_cell.reshape(1, rows),
        lattice_frac,
        dres_dx,
        dobj_dx,
    )
    got = lax.all_to_all(packed, "blk", 0, 0, tiled=True)

    residual = pl.pallas_call(
        sweep_kernel,
        out_shape=jax.ShapeDtypeStruct(adjoint.shape, F32),
        in_specs=[smem] + [vmem] * 7,
        out_specs=vmem,
        name="sweep",
    )(conv_mats.reshape(-1), adjoint, jac_diag, face_scale, kappa, source, low, high)

    box_sens = pl.pallas_call(
        sum_kernel,
        out_shape=jax.ShapeDtypeStruct((3, LAT**3), F32),
        in_specs=[vmem],
        out_specs=vmem,
        name="sum_rows",
    )(got)
    return residual, box_sens


def solution(mesh):
    in_specs = (
        P("group", "blk", None, None),
        P("group", None, "blk", None, None),
        P(),
        P("group", "blk", None, None),
        P(("group", "blk"), None, None),
        P("group", "blk", None, None),
        P(("group", "blk"), None),
        P(("group", "blk")),
        P(None, ("group", "blk")),
        P(None, None, ("group", "blk")),
        P(None, ("group", "blk")),
    )
    out_specs = (P("group", "blk", None, None), P("group", "blk"))
    return jax.shard_map(local, mesh=mesh, in_specs=in_specs, out_specs=out_specs, check_vma=False)
```

time: 465 us -> 27.5 us (0.06)
  the two profiles are of different devices: /device:TPU:0 before, /device:TPU:8 now
where the time goes in v1:
time: 27.5 us; the launch traced here: 27.1 us
  starting transfers between devices  11.3 us (41%)
  Pallas kernels  8.92 us (32%)
  waiting for transfers between devices  2.84 us (10%)
  local copies, waits for them, and re-layouts  2.54 us (9%)
  other arithmetic  0.78 us (3%)
  between operations  0.66 us (2%)
    all_to_all x1, starting transfers between devices, local(): got = lax.all_to_all(packed, 'blk', 0, 0, tiled=True)  6.3 us
    pallas_call x1, Pallas kernels, local(): pl.pallas_call(sweep_kernel, out_shape=jax.ShapeDtypeStruct(adjoint.shape...  3.4 us
    ppermute x1, starting transfers between devices, local(): lax.ppermute(stacked[:, :1], 'blk', [(i + 1, i) for i in range(ends)])  3.11 us
    pallas_call x1, Pallas kernels, local(): pl.pallas_call(sum_kernel, out_shape=jax.ShapeDtypeStruct((3, LAT ** 3),...  2.99 us
    ppermute x1, waiting for transfers between devices, local(): lax.ppermute(stacked[:, -1:], 'blk', [(i, i + 1) for i in range(ends)])  2.83 us
    pallas_call x1, Pallas kernels, local(): pl.pallas_call(functools.partial(pack_kernel, boxes, cap), out_shape=jax....  2.54 us
    unnamed x7, local copies, waits for them, and re-layouts  1.97 us
    ppermute x1, starting transfers between devices, local(): lax.ppermute(stacked[:, -1:], 'blk', [(i, i + 1) for i in range(ends)])  1.92 us
  transfers between devices with their start and end apart: 3, of which 1 were waited for; matrix products, arithmetic and copies ran while one was open for 8% of the time, Pallas kernels for 13%

profile of v1, /device:TPU:8, one launch (start us, length us, event | category | flops | bytes accessed | tf_op | source)
XLA Modules:
  0.0 27.1 jit_solution(18307589761740082604)
XLA Ops:
  0.6 2.5 %pack_rows.1 = f32[16,8,256]{2,1,0:T(8,128)} custom-call(f32[5,16,8,128]{3,2,1,0:T(8,128)} %adj_ref.3, s32[1,2048]{1,0:T(1,128)} %bitcast.4, s32[1,2048]{1,0:T(1,128)} %bitcast.5, f32[3,2048]{1,0:T(4,128)} %frac_ref.1, f32[5,3,2048]{2,1,0:T(4,128)} %dres_ref.1, f32[3,2048]{1,0:T(4,128)} %dobj_ref.1), custom_call_target="tpu_custom_call" | custom-call | tf_op jit(solution)/shard_map/pack_rows/pallas_call | solution.py:178
  3.2 6.3 %all-to-all-start = ((f32[16,8,256]{2,1,0:T(8,128)}), f32[16,8,256]{2,1,0:T(8,128)S(1)}, u32[]{:S(2)}, u32[]{:S(2)}) async-start(f32[16,8,256]{2,1,0:T(8,128)} %pack_rows.1), calls=%async_computation | async-start | bytes 262144 | tf_op jit(solution)/shard_map/all_to_all | solution.py:193
  9.5 0.8 %pad_maximum_fusion = (f32[6,1,8,128]{3,2,1,0:T(8,128)S(1)}, f32[6,1,8,128]{3,2,1,0:T(8,128)S(1)}) fusion(f32[1,16,8,128]{3,2,1,0:T(8,128)} %bitcast.3, f32[5,16,8,128]{3,2,1,0:T(8,128)} %adj_ref.3), kind=kLoop, calls=%fused_computation | loop fusion | flops 12288 | bytes 442368 | tf_op jit(solution)/shard_map/concatenate | solution.py:174
  10.3 3.1 %collective-permute-start.1 = (f32[6,1,8,128]{3,2,1,0:T(8,128)S(1)}, f32[6,1,8,128]{3,2,1,0:T(8,128)S(1)}, u32[]{:S(2)}, u32[]{:S(2)}) collective-permute-start(f32[6,1,8,128]{3,2,1,0:T(8,128)S(1)} %get-tuple-element.2), channel_id=1, source_target_pairs={{1,0},{2,1},{3,2},{4,3},{5,4},{6,5},{7,6},{8,7},{9,8},{10,9},{11,1... | collective-permute-start | bytes 73736 | tf_op jit(solution)/shard_map/ppermute | solution.py:176
  13.4 1.9 %collective-permute-start = (f32[6,1,8,128]{3,2,1,0:T(8,128)S(1)}, f32[6,1,8,128]{3,2,1,0:T(8,128)S(1)}, u32[]{:S(2)}, u32[]{:S(2)}) collective-permute-start(f32[6,1,8,128]{3,2,1,0:T(8,128)S(1)} %get-tuple-element.3), channel_id=1, source_target_pairs={{0,1},{1,2},{2,3},{3,4},{4,5},{5,6},{6,7},{7,8},{8,9},{9,10},{10,1... | collective-permute-start | bytes 73736 | tf_op jit(solution)/shard_map/ppermute | solution.py:175
  15.3 0.7 %copy.14 = f32[3,5,5]{2,1,0:T(8,128)S(1)} copy(f32[3,5,5]{2,0,1:T(4,128)} %param.13) | data formatting | bytes 600 | tf_op args[2]
  16.0 0.6 %reshape.13.conv_ref = f32[75]{0:T(128)} reshape(f32[3,5,5]{2,1,0:T(8,128)S(1)} %copy.14) | data formatting | bytes 600 | tf_op jit(solution)/shard_map/reshape | solution.py:201
  16.6 0.0 collective-permute-done.1.high_ref
  16.6 0.0 copy-start.1
  16.6 2.8 %collective-permute-done.low_ref = f32[6,1,8,128]{3,2,1,0:T(8,128)S(1)} collective-permute-done((f32[6,1,8,128]{3,2,1,0:T(8,128)S(1)}, f32[6,1,8,128]{3,2,1,0:T(8,128)S(1)}, u32[]{:S(2)}, u32[]{:S(2)}) %collective-permute-start) | collective-permute-done | bytes 24608 | tf_op jit(solution)/shard_map/ppermute | solution.py:175
  19.4 0.0 copy-done.1
  19.4 0.0 copy-start.2
  19.4 0.6 %copy-done.2 = f32[6,1,8,128]{3,2,1,0:T(8,128)} copy-done((f32[6,1,8,128]{3,2,1,0:T(8,128)}, f32[6,1,8,128]{3,2,1,0:T(8,128)S(1)}, u32[]{:S(2)}) %copy-start.2) | copy-done | bytes 24600
  20.0 3.4 %sweep.1 = f32[5,16,8,128]{3,2,1,0:T(8,128)} custom-call(f32[75]{0:T(128)} %reshape.13.conv_ref, f32[5,16,8,128]{3,2,1,0:T(8,128)} %adj_ref.3, f32[5,5,16,8,128]{4,3,2,1,0:T(8,128)} %jac_ref.1, f32[3,16,8,128]{3,2,1,0:T(8,128)} %face_ref.1, f32[16,8,128]{2,1,0:T(8,128)} %kap_ref.1, f32[5,16,8,128]{3,2,1,0:T(8,128)} %src_ref.1, f32[6,1,8,128]{3,2,1,0:T(8,128)} %copy-done.2, ...), custom_call_target="tpu_custom_call" | custom-call | tf_op jit(solution)/shard_map/sweep/pallas_call | solution.py:195
  23.4 0.0 all-to-all-done.got_ref
  23.4 0.0 copy-start
  23.4 0.7 %copy-done = f32[16,8,256]{2,1,0:T(8,128)} copy-done((f32[16,8,256]{2,1,0:T(8,128)}, f32[16,8,256]{2,1,0:T(8,128)S(1)}, u32[]{:S(2)}) %copy-start) | copy-done | bytes 131096
  24.1 3.0 %sum_rows.1 = f32[3,4096]{1,0:T(4,128)} custom-call(f32[16,8,256]{2,1,0:T(8,128)} %copy-done), custom_call_target="tpu_custom_call" | custom-call | tf_op jit(solution)/shard_map/sum_rows/pallas_call | solution.py:203
Async XLA Ops:
  3.2 20.3 %all-to-all-start = ((f32[16,8,256]{2,1,0:T(8,128)}), f32[16,8,256]{2,1,0:T(8,128)S(1)}, u32[]{:S(2)}, u32[]{:S(2)}) async-start(f32[16,8,256]{2,1,0:T(8,128)} %pack_rows.1), calls=%async_computation | async-start | bytes 262144 | tf_op jit(solution)/shard_map/all_to_all | solution.py:193
  10.3 6.3 %collective-permute-start.1 = (f32[6,1,8,128]{3,2,1,0:T(8,128)S(1)}, f32[6,1,8,128]{3,2,1,0:T(8,128)S(1)}, u32[]{:S(2)}, u32[]{:S(2)}) collective-permute-start(f32[6,1,8,128]{3,2,1,0:T(8,128)S(1)} %get-tuple-element.2), channel_id=1, source_target_pairs={{1,0},{2,1},{3,2},{4,3},{5,4},{6,5},{7,6},{8,7},{9,8},{10,9},{11,1... | collective-permute-start | bytes 73736 | tf_op jit(solution)/shard_map/ppermute | solution.py:176
  13.4 6.0 %collective-permute-start = (f32[6,1,8,128]{3,2,1,0:T(8,128)S(1)}, f32[6,1,8,128]{3,2,1,0:T(8,128)S(1)}, u32[]{:S(2)}, u32[]{:S(2)}) collective-permute-start(f32[6,1,8,128]{3,2,1,0:T(8,128)S(1)} %get-tuple-element.3), channel_id=1, source_target_pairs={{0,1},{1,2},{2,3},{3,4},{4,5},{5,6},{6,7},{7,8},{8,9},{9,10},{10,1... | collective-permute-start | bytes 73736 | tf_op jit(solution)/shard_map/ppermute | solution.py:175
  16.6 2.8 %copy-start.1 = (f32[6,1,8,128]{3,2,1,0:T(8,128)}, f32[6,1,8,128]{3,2,1,0:T(8,128)S(1)}, u32[]{:S(2)}) copy-start(f32[6,1,8,128]{3,2,1,0:T(8,128)S(1)} %collective-permute-done.1.high_ref) | copy-start | bytes 73732
  19.4 0.6 %copy-start.2 = (f32[6,1,8,128]{3,2,1,0:T(8,128)}, f32[6,1,8,128]{3,2,1,0:T(8,128)S(1)}, u32[]{:S(2)}) copy-start(f32[6,1,8,128]{3,2,1,0:T(8,128)S(1)} %collective-permute-done.low_ref) | copy-start | bytes 73732
  23.4 0.7 %copy-start = (f32[16,8,256]{2,1,0:T(8,128)}, f32[16,8,256]{2,1,0:T(8,128)S(1)}, u32[]{:S(2)}) copy-start(f32[16,8,256]{2,1,0:T(8,128)S(1)} %all-to-all-done.got_ref) | copy-start | bytes 393220

commit v2 on v1

--- a/solution.py
+++ b/solution.py
@@ -9,6 +9,7 @@
 
 LAT = 16
 CHUNK = 256
+SMALL = 12 * 2**20
 F32 = jnp.float32
 BF16 = jnp.bfloat16
 NT = (((1,), (1,)), ((), ()))
@@ -21,9 +22,121 @@
     return hi, lo
 
 
-def pack_kernel(boxes, cap, adj_ref, box_ref, cell_ref, frac_ref, dres_ref, dobj_ref, out_ref, ranks_ref):
-    fields, planes, _, lanes = adj_ref.shape
+def on_even():
+    return lax.axis_index("blk") % 2 == 0
+
+
+def stay(*arrays):
+    return [pltpu.with_memory_space_constraint(a, pltpu.HBM) for a in arrays]
+
+
+def start_all(copies):
+    for copy in copies:
+        copy.start()
+    return copies
+
+
+def wait_all(copies):
+    for copy in copies:
+        copy.wait()
+
+
+def halo_kernel(adj_hbm, kap_hbm, mate_ref, other_ref, sems):
+    fields, planes = adj_hbm.shape[:2]
+    even = (lax.axis_index("blk") + 1) % 2
+    copies = []
+    for i, (ref, x) in enumerate(
+        ((mate_ref, even * (planes - 1)), (other_ref, (1 - even) * (planes - 1)))
+    ):
+        copies.append(
+            pltpu.make_async_copy(adj_hbm.at[:, x], ref.at[pl.ds(0, fields)], sems.at[2 * i])
+        )
+        copies.append(pltpu.make_async_copy(kap_hbm.at[x], ref.at[fields], sems.at[2 * i + 1]))
+    wait_all(start_all(copies))
+
+
+def plane_residual(psi, kap, below, above, jac, face, src, conv):
+    fields = len(psi)
+    rows, lanes = kap.shape
+    row = lax.broadcasted_iota(jnp.int32, (rows, lanes), 0)
+    lane = lax.broadcasted_iota(jnp.int32, (rows, lanes), 1)
+    masks = ((row < rows - 1, row > 0), (lane < lanes - 1, lane > 0))
+
+    def sides(value, dim):
+        size = value.shape[dim]
+        up = jnp.where(masks[dim][0], pltpu.roll(value, size - 1, dim), 0.0)
+        down = jnp.where(masks[dim][1], pltpu.roll(value, 1, dim), 0.0)
+        return up, down
+
+    centre = list(psi) + [kap]
+    result = []
+    for f in range(fields):
+        total = jac(0, f) * psi[0]
+        for k in range(1, fields):
+            total = total + jac(k, f) * psi[k]
+        result.append(total - src(f))
+    spread = None
+    for d in range(3):
+        pair = list(zip(above, below)) if d == 0 else [sides(v, d - 1) for v in centre]
+        scale = 0.5 * face(d)
+        diff = [scale * (pair[k][0] - pair[k][1]) for k in range(fields)]
+        up = 0.5 * (kap + pair[fields][0])
+        down = 0.5 * (kap + pair[fields][1])
+        spread = up + down if spread is None else spread + up + down
+        for f in range(fields):
+            total = result[f]
+            for k in range(fields):
+                total = total + conv[k, d, f] * diff[k]
+            result[f] = total - up * pair[f][0] - down * pair[f][1]
+    return [result[f] + spread * psi[f] for f in range(fields)]
+
+
+def work_kernel(
+    boxes,
+    cap,
+    adj_hbm,
+    jac_hbm,
+    conv_hbm,
+    face_hbm,
+    kap_hbm,
+    src_hbm,
+    box_hbm,
+    cell_hbm,
+    frac_hbm,
+    dres_hbm,
+    dobj_hbm,
+    mate_hbm,
+    other_hbm,
+    out_ref,
+    res_hbm,
+    adj_ref,
+    jac_ref,
+    conv_ref,
+    face_ref,
+    kap_ref,
+    src_ref,
+    box_ref,
+    cell_ref,
+    frac_ref,
+    dres_ref,
+    dobj_ref,
+    mate_ref,
+    other_ref,
+    ranks_ref,
+    res_ref,
+    sems,
+    out_sems,
+):
+    fields, planes, _, lanes = adj_hbm.shape
     rows = planes * lanes
+    moves = [(box_hbm, box_ref), (dres_hbm, dres_ref), (adj_hbm, adj_ref)]
+    moves += [(dobj_hbm, dobj_ref), (frac_hbm, frac_ref), (cell_hbm, cell_ref)]
+    moves += [(kap_hbm, kap_ref), (conv_hbm, conv_ref), (jac_hbm, jac_ref)]
+    moves += [(src_hbm, src_ref), (face_hbm, face_ref), (mate_hbm, mate_ref), (other_hbm, other_ref)]
+    copies = start_all(
+        [pltpu.make_async_copy(src, dst, sems.at[i]) for i, (src, dst) in enumerate(moves)]
+    )
+    copies[0].wait()
     box = box_ref[...]
 
     chunks = rows // CHUNK
@@ -44,6 +157,7 @@
         )
         offset = offset + here[:, CHUNK - 1:] + hot[j][:, CHUNK - 1:]
 
+    wait_all(copies[1:6])
     total = jnp.zeros((boxes * 16, cap), F32)
     slots = lax.broadcasted_iota(jnp.int32, (cap, CHUNK), 0).astype(F32)
     per = CHUNK // lanes
@@ -68,6 +182,38 @@
         total = total + lax.dot_general(lhs, rhs, NT, preferred_element_type=F32)
     for b in range(boxes):
         out_ref[b] = total[b * 16:b * 16 + 8] + total[b * 16 + 8:b * 16 + 16]
+
+    wait_all(copies[6:])
+    even = on_even()
+    sent = []
+    steps = 4
+    for i in range(steps):
+        p = slice(planes * i // steps, planes * (i + 1) // steps)
+        for x in range(p.start, p.stop):
+            def at(y):
+                if 0 <= y < planes:
+                    return [adj_ref[f, y] for f in range(fields)] + [kap_ref[y]]
+                return [
+                    jnp.where(even == (y < 0), other_ref[f], mate_ref[f]) for f in range(fields + 1)
+                ]
+
+            here = at(x)
+            planes_of = plane_residual(
+                here[:fields],
+                here[fields],
+                at(x - 1),
+                at(x + 1),
+                lambda k, f: jac_ref[k, f, x],
+                lambda d: face_ref[d, x],
+                lambda f: src_ref[f, x],
+                conv_ref,
+            )
+            for f in range(fields):
+                res_ref[f, x] = planes_of[f]
+        copy = pltpu.make_async_copy(res_ref.at[:, p], res_hbm.at[:, p], out_sems.at[i])
+        copy.start()
+        sent.append(copy)
+    wait_all(sent)
 
 
 def sum_kernel(got_ref, out_ref):
@@ -101,56 +247,6 @@
             out_ref[c:c + 1, a * LAT * LAT:(a + 1) * LAT * LAT] = result[c * LAT + a:c * LAT + a + 1]
 
 
-def sweep_kernel(conv_ref, adj_ref, jac_ref, face_ref, kap_ref, src_ref, low_ref, high_ref, out_ref):
-    fields, planes, rows, lanes = adj_ref.shape
-    row = lax.broadcasted_iota(jnp.int32, (rows, lanes), 0)
-    lane = lax.broadcasted_iota(jnp.int32, (rows, lanes), 1)
-    keep = (
-        (row < rows - 1, row > 0),
-        (lane < lanes - 1, lane > 0),
-    )
-
-    def at(field, x):
-        if x < 0:
-            return low_ref[field, 0]
-        if x == planes:
-            return high_ref[field, 0]
-        return adj_ref[field, x] if field < fields else kap_ref[x]
-
-    def shifted(value, dim):
-        size = value.shape[dim]
-        up = jnp.where(keep[dim][0], pltpu.roll(value, size - 1, dim), 0.0)
-        down = jnp.where(keep[dim][1], pltpu.roll(value, 1, dim), 0.0)
-        return up, down
-
-    for x in range(planes):
-        centre = [at(f, x) for f in range(fields)]
-        kap = at(fields, x)
-        result = []
-        for f in range(fields):
-            total = jac_ref[0, f, x] * centre[0]
-            for k in range(1, fields):
-                total = total + jac_ref[k, f, x] * centre[k]
-            result.append(total - src_ref[f, x])
-        for direction in range(3):
-            if direction == 0:
-                pair = [(at(f, x + 1), at(f, x - 1)) for f in range(fields + 1)]
-            else:
-                pair = [shifted(v, direction - 1) for v in centre + [kap]]
-            scale = 0.5 * face_ref[direction, x]
-            diff = [scale * (pair[k][0] - pair[k][1]) for k in range(fields)]
-            up = 0.5 * (kap + pair[fields][0])
-            down = 0.5 * (kap + pair[fields][1])
-            for f in range(fields):
-                total = result[f]
-                for k in range(fields):
-                    total = total + conv_ref[(direction * fields + k) * fields + f] * diff[k]
-                total = total - up * (pair[f][0] - centre[f]) - down * (pair[f][1] - centre[f])
-                result[f] = total
-        for f in range(fields):
-            out_ref[f, x] = result[f]
-
-
 def local(
     adjoint,
     jac_diag,
@@ -167,44 +263,86 @@
     boxes = lax.axis_size("blk")
     rows = box_of_row.shape[0]
     cap = 2 * rows // boxes
+    fields, planes = adjoint.shape[:2]
+    plane = adjoint.shape[2:]
     vmem = pl.BlockSpec(memory_space=pltpu.VMEM)
-    smem = pl.BlockSpec(memory_space=pltpu.SMEM)
-
-    ends = boxes - 1
-    stacked = jnp.concatenate([adjoint, kappa[None]], 0)
-    low = lax.ppermute(stacked[:, -1:], "blk", [(i, i + 1) for i in range(ends)])
-    high = lax.ppermute(stacked[:, :1], "blk", [(i + 1, i) for i in range(ends)])
-
-    packed = pl.pallas_call(
-        functools.partial(pack_kernel, boxes, cap),
-        out_shape=jax.ShapeDtypeStruct((boxes, 8, cap), F32),
-        in_specs=[vmem] * 6,
-        out_specs=vmem,
-        scratch_shapes=[pltpu.VMEM((1, rows), F32)],
-        name="pack_rows",
+    hbm = pl.BlockSpec(memory_space=pltpu.HBM)
+    params = pltpu.CompilerParams(vmem_limit_bytes=SMALL)
+    conv = conv_mats.transpose(1, 0, 2)
+    box_row = box_of_row.reshape(1, rows)
+    cell_row = lattice_cell.reshape(1, rows)
+    box_row, cell_row, conv, adjoint, jac_diag, face_scale, kappa, source = stay(
+        box_row, cell_row, conv, adjoint, jac_diag, face_scale, kappa, source
+    )
+    lattice_frac, dres_dx, dobj_dx = stay(lattice_frac, dres_dx, dobj_dx)
+
+    def shape(*dims):
+        return jax.ShapeDtypeStruct(dims, F32)
+
+    halo = (fields + 1,) + plane
+    to_mate, to_other = pl.pallas_call(
+        halo_kernel,
+        out_shape=(shape(*halo), shape(*halo)),
+        in_specs=[hbm, hbm],
+        out_specs=(vmem, vmem),
+        scratch_shapes=[pltpu.SemaphoreType.DMA((4,))],
+        compiler_params=params,
+        name="halo_planes",
+    )(adjoint, kappa)
+    pairs = [(i, i + 1) for i in range(boxes - 1)]
+    both_ways = [[p for i, j in pairs if i % 2 == turn for p in ((i, j), (j, i))] for turn in (0, 1)]
+    mate = lax.ppermute(to_mate, "blk", both_ways[0])
+    other = lax.ppermute(to_other, "blk", both_ways[1])
+
+    packed, residual = pl.pallas_call(
+        functools.partial(work_kernel, boxes, cap),
+        out_shape=(shape(boxes, 8, cap), shape(*adjoint.shape)),
+        in_specs=[hbm] * 11 + [pl.BlockSpec(memory_space=pl.ANY)] * 2,
+        out_specs=(vmem, hbm),
+        scratch_shapes=[
+            pltpu.VMEM(adjoint.shape, F32),
+            pltpu.VMEM(jac_diag.shape, F32),
+            pltpu.SMEM(conv.shape, F32),
+            pltpu.VMEM(face_scale.shape, F32),
+            pltpu.VMEM(kappa.shape, F32),
+            pltpu.VMEM(source.shape, F32),
+            pltpu.VMEM((1, rows), jnp.int32),
+            pltpu.VMEM((1, rows), jnp.int32),
+            pltpu.VMEM(lattice_frac.shape, F32),
+            pltpu.VMEM(dres_dx.shape, F32),
+            pltpu.VMEM(dobj_dx.shape, F32),
+            pltpu.VMEM(halo, F32),
+            pltpu.VMEM(halo, F32),
+            pltpu.VMEM((1, rows), F32),
+            pltpu.VMEM(adjoint.shape, F32),
+            pltpu.SemaphoreType.DMA((13,)),
+            pltpu.SemaphoreType.DMA((4,)),
+        ],
+        compiler_params=params,
+        name="pack_and_sweep",
     )(
         adjoint,
-        box_of_row.reshape(1, rows),
-        lattice_cell.reshape(1, rows),
+        jac_diag,
+        conv,
+        face_scale,
+        kappa,
+        source,
+        box_row,
+        cell_row,
         lattice_frac,
         dres_dx,
         dobj_dx,
+        mate,
+        other,
     )
     got = lax.all_to_all(packed, "blk", 0, 0, tiled=True)
-
-    residual = pl.pallas_call(
-        sweep_kernel,
-        out_shape=jax.ShapeDtypeStruct(adjoint.shape, F32),
-        in_specs=[smem] + [vmem] * 7,
-        out_specs=vmem,
-        name="sweep",
-    )(conv_mats.reshape(-1), adjoint, jac_diag, face_scale, kappa, source, low, high)
 
     box_sens = pl.pallas_call(
         sum_kernel,
-        out_shape=jax.ShapeDtypeStruct((3, LAT**3), F32),
+        out_shape=shape(3, LAT**3),
         in_specs=[vmem],
         out_specs=vmem,
+        compiler_params=params,
         name="sum_rows",
     )(got)
     return residual, box_sens

time: 27.5 us -> 27.7 us (level)
  the two profiles are of different devices: /device:TPU:8 before, /device:TPU:0 now
where the time goes in v2:
time: 27.7 us; the launch traced here: 27.4 us
  blocking collectives  19 us (69%)
  Pallas kernels  6.42 us (23%)
  starting transfers between devices  1.17 us (4%)
  between operations  0.65 us (2%)
    all_to_all x1, blocking collectives, local(): got = lax.all_to_all(packed, 'blk', 0, 0, tiled=True)  19 us
    pallas_call x1, Pallas kernels, local(): pl.pallas_call(functools.partial(work_kernel, boxes, cap), out_shape=(sha...  3.52 us
    pallas_call x1, Pallas kernels, local(): pl.pallas_call(sum_kernel, out_shape=shape(3, LAT ** 3), in_specs=[vmem],...  2.08 us
    pallas_call x1, Pallas kernels, local(): pl.pallas_call(halo_kernel, out_shape=(shape(*halo), shape(*halo)), in_sp...  0.81 us
    ppermute x1, starting transfers between devices, local(): other = lax.ppermute(to_other, 'blk', both_ways[1])  0.65 us
  transfers between devices with their start and end apart: 2, of which 1 were waited for; matrix products, arithmetic and copies ran while one was open for 0% of the time, Pallas kernels for 0%

profile of v2, /device:TPU:0, one launch (start us, length us, event | category | flops | bytes accessed | tf_op | source)
XLA Modules:
  0.0 27.4 jit_solution(8566606194593708175)
XLA Ops:
  0.6 0.8 %halo_planes.1 = (f32[6,8,128]{2,1,0:T(8,128)S(1)}, f32[6,8,128]{2,1,0:T(8,128)S(1)}) custom-call(f32[5,16,8,128]{3,2,1,0:T(8,128)} %adj_hbm.3, f32[16,8,128]{2,1,0:T(8,128)} %kap_hbm.3), custom_call_target="tpu_custom_call" | custom-call | tf_op jit(solution)/shard_map/halo_planes/pallas_call | solution.py:283
  1.4 0.5 %collective-permute-start = (f32[6,8,128]{2,1,0:T(8,128)S(1)}, f32[6,8,128]{2,1,0:T(8,128)S(1)}, u32[]{:S(2)}, u32[]{:S(2)}) collective-permute-start(f32[6,8,128]{2,1,0:T(8,128)S(1)} %get-tuple-element.6), channel_id=1, source_target_pairs={{0,1},{1,0},{2,3},{3,2},{4,5},{5,4},{6,7},{7,6},{8,9},{9,8},{10,11... | collective-permute-start | bytes 73736 | tf_op jit(solution)/shard_map/ppermute | solution.py:294
  2.0 0.7 %collective-permute-start.1 = (f32[6,8,128]{2,1,0:T(8,128)S(1)}, f32[6,8,128]{2,1,0:T(8,128)S(1)}, u32[]{:S(2)}, u32[]{:S(2)}) collective-permute-start(f32[6,8,128]{2,1,0:T(8,128)S(1)} %get-tuple-element.7), channel_id=1, source_target_pairs={{1,2},{2,1},{3,4},{4,3},{5,6},{6,5},{7,8},{8,7},{9,10},{10,9},{11,... | collective-permute-start | bytes 73736 | tf_op jit(solution)/shard_map/ppermute | solution.py:295
  2.6 0.2 collective-permute-done.mate_hbm
  2.8 0.0 collective-permute-done.1.other_hbm
  2.8 3.5 %pack_and_sweep.1 = (f32[16,8,256]{2,1,0:T(8,128)S(1)}, f32[5,16,8,128]{3,2,1,0:T(8,128)}) custom-call(f32[5,16,8,128]{3,2,1,0:T(8,128)} %adj_hbm.3, f32[5,5,16,8,128]{4,3,2,1,0:T(8,128)} %jac_hbm.1, f32[5,3,5]{2,1,0:T(4,128)} %bitcast.3, f32[3,16,8,128]{3,2,1,0:T(8,128)} %face_hbm.1, f32[16,8,128]{2,1,0:T(8,128)} %kap_hbm.3, f32[5,16,8,128]{3,2,1,0:T(8,128)} %src_hbm.1, ...), custom_call_target="tpu_custom_call" | custom-call | tf_op jit(solution)/shard_map/pack_and_sweep/pallas_call | solution.py:297
  6.3 19.0 %all_to_all.5.got_ref = f32[16,8,256]{2,1,0:T(8,128)S(1)} all-to-all(f32[16,8,256]{2,1,0:T(8,128)S(1)} %get-tuple-element.9), channel_id=1, replica_groups=mesh['group'=2,'blk'=16] {'blk'}, dimensions={0} | all-to-all | bytes 262144 | tf_op jit(solution)/shard_map/all_to_all | solution.py:338
  25.3 2.1 %sum_rows.1 = f32[3,4096]{1,0:T(4,128)} custom-call(f32[16,8,256]{2,1,0:T(8,128)S(1)} %all_to_all.5.got_ref), custom_call_target="tpu_custom_call" | custom-call | tf_op jit(solution)/shard_map/sum_rows/pallas_call | solution.py:340
Async XLA Ops:
  1.4 1.4 %collective-permute-start = (f32[6,8,128]{2,1,0:T(8,128)S(1)}, f32[6,8,128]{2,1,0:T(8,128)S(1)}, u32[]{:S(2)}, u32[]{:S(2)}) collective-permute-start(f32[6,8,128]{2,1,0:T(8,128)S(1)} %get-tuple-element.6), channel_id=1, source_target_pairs={{0,1},{1,0},{2,3},{3,2},{4,5},{5,4},{6,7},{7,6},{8,9},{9,8},{10,11... | collective-permute-start | bytes 73736 | tf_op jit(solution)/shard_map/ppermute | solution.py:294
  2.0 0.9 %collective-permute-start.1 = (f32[6,8,128]{2,1,0:T(8,128)S(1)}, f32[6,8,128]{2,1,0:T(8,128)S(1)}, u32[]{:S(2)}, u32[]{:S(2)}) collective-permute-start(f32[6,8,128]{2,1,0:T(8,128)S(1)} %get-tuple-element.7), channel_id=1, source_target_pairs={{1,2},{2,1},{3,4},{4,3},{5,6},{6,5},{7,8},{8,7},{9,10},{10,9},{11,... | collective-permute-start | bytes 73736 | tf_op jit(solution)/shard_map/ppermute | solution.py:295
